TPU v7x, 32 devices: a whole 2x2x4 slice. The times are simulated.
32 devices in a mesh: dp: 16 (over z, y, core), fsdp: 2 (over x).
Axes of the slice: x: 2, y: 2, z: 4, core: 2. Of those that a mesh axis runs over, the one named last changes fastest.
Arguments:
- acts: bfloat16 [2, 32, 512, 1024], P(None, ('dp', 'fsdp')), may hold values from -6 to 6
- cotangent: bfloat16 [2, 32, 512, 1024], P(None, ('dp', 'fsdp')), may hold values from -6 to 6
- seg_ids: int32 [2, 32, 512], P(None, ('dp', 'fsdp')), may hold values from 0 to 7, never falling along the last dimension, each value on 1 to 256 neighbouring positions
- pad_mask: int32 [2, 32, 512], P(None, ('dp', 'fsdp')), may hold values from 0 to 1, as said below
- qkv_weight: bfloat16 [1024, 3072], P('fsdp', 'dp')
- out_weight: bfloat16 [1024, 1024], P('fsdp', 'dp'), may hold values from -0.1875 to 0.1875
- in_weight: bfloat16 [1024, 4096], P('fsdp', 'dp'), may hold values from -0.1875 to 0.1875
- down_weight: bfloat16 [4096, 1024], P('fsdp', 'dp'), may hold values from -0.1875 to 0.1875
- biases: float32 [12288], replicated
- moment_first: float32 [2, 6, 32, 32], P('fsdp'), as said below
- moment_second: float32 [2, 6, 32, 32], P('fsdp'), as said below
- basis_left: float32 [2, 6, 32, 32], P('fsdp'), as said below
- basis_right: float32 [2, 6, 32, 32], P('fsdp'), as said below
- owners: int32 [12], replicated, may hold values from 0 to 1, as said below
Outputs:
- out_acts: bfloat16 [2, 32, 512, 1024], P(None, ('dp', 'fsdp'))
- in_grad: bfloat16 [2, 32, 512, 1024], P(None, ('dp', 'fsdp'))
- bias_grad: float32 [12288], replicated
- moment_first_new: float32 [2, 6, 32, 32], P('fsdp')
- moment_second_new: float32 [2, 6, 32, 32], P('fsdp')
- bias_new: float32 [12288], replicated
- bias_low: bfloat16 [12288], replicated
Inputs may be any that keep to these rules, and one draw needn't show every extreme that they name: `seg_ids`: never falling along a slot. `pad_mask`: in each slot the ones are a prefix of 384 to 512 positions and the zeros fill the rest. `owners`: every fsdp index owns at most 6 blocks and some own exactly 6. `moment_first`: slot (f, c) holds the block that owner f holds at rank c; other slots are ignored. `moment_second`: Positive; slots as in moment_first. `basis_left`: each slot is an orthogonal matrix; slots as in moment_first. `basis_right`: each slot is an orthogonal matrix; slots as in moment_first.
All inputs are finite; a program needn't handle non-finite values.
Results may differ from a plain program's by a relative error of at most 0.017.
Values may be sent and summed in bfloat16 or wider, within the bound.
A program may use at most 192 MiB of HBM per device.

v0:
```python
import math

import jax
import jax.numpy as jnp
from jax import lax
from jax.sharding import PartitionSpec as P

D = 1024
H = 16
HD = 64
FF = 4096
SEQ = 512
MB = 2
STEP = 5


norm_eps = 1e-12
precise = lax.Precision.HIGHEST
decay_first = 0.5
decay_second = 0.5
adam_eps = 1e-08
step_rate = 0.4


def gather_attention(qkv_shard, out_shard):
    qkv_rows, out_rows = (
        lax.all_gather(qkv_shard, "fsdp", axis=0, tiled=True),
        lax.all_gather(out_shard, "fsdp", axis=0, tiled=True),
    )
    return (
        lax.all_gather(qkv_rows, "dp", axis=1, tiled=True),
        lax.all_gather(out_rows, "dp", axis=1, tiled=True),
    )


def gather_feed(in_shard, down_shard):
    in_rows, down_rows = (
        lax.all_gather(in_shard, "fsdp", axis=0, tiled=True),
        lax.all_gather(down_shard, "fsdp", axis=0, tiled=True),
    )
    return (
        lax.all_gather(in_rows, "dp", axis=1, tiled=True),
        lax.all_gather(down_rows, "dp", axis=1, tiled=True),
    )


def gather_attention_back(qkv_shard, out_shard):
    qkv_rows, out_rows = (
        lax.all_gather(qkv_shard, "fsdp", axis=0, tiled=True),
        lax.all_gather(out_shard, "fsdp", axis=0, tiled=True),
    )
    return (
        lax.all_gather(qkv_rows, "dp", axis=1, tiled=True),
        lax.all_gather(out_rows, "dp", axis=1, tiled=True),
    )


def gather_feed_back(in_shard, down_shard):
    in_rows, down_rows = (
        lax.all_gather(in_shard, "fsdp", axis=0, tiled=True),
        lax.all_gather(down_shard, "fsdp", axis=0, tiled=True),
    )
    return (
        lax.all_gather(in_rows, "dp", axis=1, tiled=True),
        lax.all_gather(down_rows, "dp", axis=1, tiled=True),
    )


def split_biases(bias_vec):
    return (
        bias_vec[0:D],
        bias_vec[D : 2 * D],
        bias_vec[2 * D : 3 * D],
        bias_vec[3 * D : 3 * D + FF],
        bias_vec[3 * D + FF : 4 * D + FF],
        bias_vec[4 * D + FF : 5 * D + FF],
        bias_vec[5 * D + FF : 6 * D + FF],
        bias_vec[6 * D + FF : 7 * D + FF],
        bias_vec[7 * D + FF : 8 * D + FF],
    )


def layer_norm_parts(values, norm_gain, norm_shift):
    centre = values - jnp.mean(values, axis=-1, keepdims=True)
    spread = jnp.mean(centre * centre, axis=-1, keepdims=True)
    inverse = lax.rsqrt(spread + norm_eps)
    normed = centre * inverse
    return (normed * norm_gain + norm_shift, normed, inverse)


def layer_norm_back(upstream, normed, inverse, norm_gain):
    gain_grad = jnp.sum(upstream * normed, axis=0)
    shift_grad = jnp.sum(upstream, axis=0)
    scaled = upstream * norm_gain
    inner_term = (
        scaled
        - jnp.mean(scaled, axis=-1, keepdims=True)
        - normed * jnp.mean(scaled * normed, axis=-1, keepdims=True)
    )
    return (inverse * inner_term, gain_grad, shift_grad)


def gelu_exact(values):
    return 0.5 * values * (1.0 + jax.scipy.special.erf(values * (1.0 / math.sqrt(2.0))))


def gelu_slope(values):
    return 0.5 * (1.0 + jax.scipy.special.erf(values * (1.0 / math.sqrt(2.0)))) + values * jnp.exp(
        -0.5 * values * values
    ) * (1.0 / math.sqrt(2.0 * math.pi))


def allowed_pairs(segment, padding):
    same_doc = segment[:, None] == segment[None, :]
    pad_query = padding[:, None] == 0
    real_key = padding[None, :] == 1
    return real_key & (same_doc | pad_query)


def slot_scores(queries, keys_all, segment, padding):
    raw_scores = jnp.einsum(
        "qhd,khd->hqk", queries, keys_all, preferred_element_type=jnp.float32
    ) * HD ** (-0.5)
    return jnp.where(allowed_pairs(segment, padding)[None], raw_scores, -1e30)


def attend_forward(operands):
    queries, keys_all, values, segment, padding = operands
    masked = slot_scores(queries, keys_all, segment, padding)
    row_peak = jnp.max(masked, axis=-1, keepdims=True)
    exponent = jnp.exp(masked - row_peak)
    row_total = jnp.sum(exponent, axis=-1, keepdims=True)
    attn_probs = (exponent / row_total).astype(jnp.bfloat16)
    context = jnp.einsum("hqk,khd->qhd", attn_probs, values, preferred_element_type=jnp.float32)
    return (context, row_peak[..., 0] + jnp.log(row_total[..., 0]))


def attend_backward(operands):
    queries, keys_all, values, segment, padding, log_total, grad_ctx = operands
    masked = slot_scores(queries, keys_all, segment, padding)
    attn_probs = jnp.exp(masked - log_total[..., None])
    probs_low = attn_probs.astype(jnp.bfloat16)
    grad_probs = jnp.einsum("qhd,khd->hqk", grad_ctx, values, preferred_element_type=jnp.float32)
    row_inner = jnp.sum(grad_probs * attn_probs, axis=-1, keepdims=True)
    grad_scores = (attn_probs * (grad_probs - row_inner)).astype(jnp.bfloat16)
    grad_query = jnp.einsum(
        "hqk,khd->qhd", grad_scores, keys_all, preferred_element_type=jnp.float32
    ) * HD ** (-0.5)
    grad_key = jnp.einsum(
        "hqk,qhd->khd", grad_scores, queries, preferred_element_type=jnp.float32
    ) * HD ** (-0.5)
    grad_value = jnp.einsum("hqk,qhd->khd", probs_low, grad_ctx, preferred_element_type=jnp.float32)
    return jnp.stack([grad_query, grad_key, grad_value], axis=1)


def layer_forward(inputs, segments, padding, attn_weights, feed_weights, biases):
    qkv_weight, out_weight = attn_weights
    in_weight, down_weight = feed_weights
    (
        query_bias,
        value_bias,
        out_bias,
        up_bias,
        down_bias,
        gain_one,
        shift_one,
        gain_two,
        shift_two,
    ) = split_biases(biases)
    slot_count = inputs.shape[0]
    token_rows = inputs.reshape(slot_count * SEQ, D)
    qkv_bias = jnp.concatenate([query_bias, jnp.zeros_like(query_bias), value_bias])
    projected = (
        jnp.dot(token_rows, qkv_weight, preferred_element_type=jnp.float32) + qkv_bias
    ).astype(jnp.bfloat16)
    shaped = projected.reshape(slot_count, SEQ, 3, H, HD)
    context, log_total = lax.map(
        attend_forward, (shaped[:, :, 0], shaped[:, :, 1], shaped[:, :, 2], segments, padding)
    )
    context_low = context.reshape(slot_count * SEQ, D).astype(jnp.bfloat16)
    branch = jnp.dot(context_low, out_weight, preferred_element_type=jnp.float32) + out_bias
    hidden, normed_one, inverse_one = layer_norm_parts(
        token_rows.astype(jnp.float32) + branch, gain_one, shift_one
    )
    hidden_low = hidden.astype(jnp.bfloat16)
    upward = jnp.dot(hidden_low, in_weight, preferred_element_type=jnp.float32) + up_bias
    activated = gelu_exact(upward).astype(jnp.bfloat16)
    feedback = jnp.dot(activated, down_weight, preferred_element_type=jnp.float32) + down_bias
    result, normed_two, inverse_two = layer_norm_parts(hidden + feedback, gain_two, shift_two)
    kept_state = (shaped, log_total, normed_one, inverse_one, upward, normed_two, inverse_two)
    return (result.reshape(slot_count, SEQ, D), kept_state)


def layer_backward(upstream, kept_state, segments, padding, attn_weights, feed_weights, biases):
    qkv_weight, out_weight = attn_weights
    in_weight, down_weight = feed_weights
    (
        query_bias,
        value_bias,
        out_bias,
        up_bias,
        down_bias,
        gain_one,
        shift_one,
        gain_two,
        shift_two,
    ) = split_biases(biases)
    shaped, log_total, normed_one, inverse_one, upward, normed_two, inverse_two = kept_state
    slot_count = upstream.shape[0]
    grad_rows = upstream.reshape(slot_count * SEQ, D).astype(jnp.float32)
    grad_pre_two, grad_gain_two, grad_shift_two = layer_norm_back(
        grad_rows, normed_two, inverse_two, gain_two
    )
    grad_feed = grad_pre_two.astype(jnp.bfloat16)
    grad_down_bias = jnp.sum(grad_feed.astype(jnp.float32), axis=0)
    grad_act = jnp.einsum("rd,fd->rf", grad_feed, down_weight, preferred_element_type=jnp.float32)
    grad_up = (grad_act * gelu_slope(upward)).astype(jnp.bfloat16)
    grad_up_bias = jnp.sum(grad_up.astype(jnp.float32), axis=0)
    grad_hidden = grad_pre_two + jnp.einsum(
        "rf,df->rd", grad_up, in_weight, preferred_element_type=jnp.float32
    )
    grad_pre_one, grad_gain_one, grad_shift_one = layer_norm_back(
        grad_hidden, normed_one, inverse_one, gain_one
    )
    grad_branch = grad_pre_one.astype(jnp.bfloat16)
    grad_out_bias = jnp.sum(grad_branch.astype(jnp.float32), axis=0)
    grad_context = jnp.einsum(
        "rd,ed->re", grad_branch, out_weight, preferred_element_type=jnp.float32
    ).astype(jnp.bfloat16)
    grad_context = grad_context.reshape(slot_count, SEQ, H, HD)
    grad_qkv = lax.map(
        attend_backward,
        (
            shaped[:, :, 0],
            shaped[:, :, 1],
            shaped[:, :, 2],
            segments,
            padding,
            log_total,
            grad_context,
        ),
    )
    grad_qkv_low = grad_qkv.reshape(slot_count * SEQ, 3 * D).astype(jnp.bfloat16)
    qkv_bias_grad = jnp.sum(grad_qkv_low.astype(jnp.float32), axis=0)
    grad_inputs = grad_pre_one + jnp.einsum(
        "re,de->rd", grad_qkv_low, qkv_weight, preferred_element_type=jnp.float32
    )
    bias_part = jnp.concatenate(
        [
            qkv_bias_grad[0:D],
            qkv_bias_grad[2 * D : 3 * D],
            grad_out_bias,
            grad_up_bias,
            grad_down_bias,
            grad_gain_one,
            grad_shift_one,
            grad_gain_two,
            grad_shift_two,
        ]
    )
    return (grad_inputs.astype(jnp.bfloat16).reshape(slot_count, SEQ, D), bias_part)


def placement_table(owners, owner_count, capacity):
    block_count = owners.shape[0]
    index_b = jnp.arange(block_count, dtype=jnp.int32)
    same_owner = owners[:, None] == owners[None, :]
    earlier = index_b[None, :] < index_b[:, None]
    rank_of = jnp.sum((same_owner & earlier).astype(jnp.int32), axis=1)
    owner_hit = owners[None, None, :] == jnp.arange(owner_count, dtype=jnp.int32)[:, None, None]
    slot_hit = rank_of[None, None, :] == jnp.arange(capacity, dtype=jnp.int32)[None, :, None]
    return (owner_hit & slot_hit).astype(jnp.float32)


def adam_rotated(grad_slots, value_slots, first_old, second_old, left_basis, right_basis, filled):
    turned = jnp.einsum("fcki,fckj->fcij", left_basis, grad_slots, precision=precise)
    turned = jnp.einsum("fcik,fckj->fcij", turned, right_basis, precision=precise)
    first_raw = decay_first * first_old + (1.0 - decay_first) * turned
    second_raw = decay_second * second_old + (1.0 - decay_second) * turned * turned
    normed_step = (
        first_raw
        / (1.0 - decay_first**STEP)
        / (jnp.sqrt(second_raw / (1.0 - decay_second**STEP)) + adam_eps)
    )
    restored = jnp.einsum("fcik,fckj->fcij", left_basis, normed_step, precision=precise)
    restored = jnp.einsum("fcik,fcjk->fcij", restored, right_basis, precision=precise)
    value_new = value_slots - step_rate * restored
    return (first_raw * filled, second_raw * filled, value_new * filled)


def body(
    acts,
    cotangent,
    seg_ids,
    pad_mask,
    qkv_weight,
    out_weight,
    in_weight,
    down_weight,
    biases,
    moment_first,
    moment_second,
    basis_left,
    basis_right,
    owners,
):
    grad_total = jnp.zeros((biases.shape[0],), jnp.float32)
    outputs = []
    input_grads = []
    for batch_index in range(MB):
        attn_now = gather_attention(qkv_weight, out_weight)
        feed_now = gather_feed(in_weight, down_weight)
        result, first_state = layer_forward(
            acts[batch_index],
            seg_ids[batch_index],
            pad_mask[batch_index],
            attn_now,
            feed_now,
            biases,
        )
        outputs.append(result.astype(jnp.bfloat16))
        attn_back = gather_attention_back(qkv_weight, out_weight)
        feed_back = gather_feed_back(in_weight, down_weight)
        result_again, kept_state = layer_forward(
            acts[batch_index],
            seg_ids[batch_index],
            pad_mask[batch_index],
            attn_back,
            feed_back,
            biases,
        )
        grad_inputs, bias_part = layer_backward(
            cotangent[batch_index],
            kept_state,
            seg_ids[batch_index],
            pad_mask[batch_index],
            attn_back,
            feed_back,
            biases,
        )
        input_grads.append(grad_inputs)
        grad_total = grad_total + bias_part
    block_count = owners.shape[0]
    block_side = moment_first.shape[2]
    slot_table = placement_table(owners, lax.axis_size("fsdp"), moment_first.shape[1])
    grad_slots = jnp.einsum(
        "fcb,bij->fcij",
        slot_table,
        grad_total.reshape(block_count, block_side, block_side),
        precision=precise,
    )
    summed = lax.psum(grad_slots.astype(jnp.bfloat16), "dp")
    owned_grad = lax.psum_scatter(summed, "fsdp", scatter_dimension=0, tiled=True).astype(
        jnp.float32
    )
    own_table = lax.dynamic_slice_in_dim(slot_table, lax.axis_index("fsdp"), 1, 0)
    value_slots = jnp.einsum(
        "fcb,bij->fcij",
        own_table,
        biases.reshape(block_count, block_side, block_side),
        precision=precise,
    )
    filled = jnp.sum(own_table, axis=2)[:, :, None, None]
    first_new, second_new, value_new = adam_rotated(
        owned_grad, value_slots, moment_first, moment_second, basis_left, basis_right, filled
    )
    shared_grad, shared_value = (
        lax.all_gather(owned_grad, "fsdp", axis=0, tiled=True),
        lax.all_gather(value_new, "fsdp", axis=0, tiled=True),
    )
    bias_grad = jnp.einsum("fcb,fcij->bij", slot_table, shared_grad, precision=precise).reshape(
        biases.shape[0]
    )
    bias_new = jnp.einsum("fcb,fcij->bij", slot_table, shared_value, precision=precise).reshape(
        biases.shape[0]
    )
    return (
        jnp.stack(outputs),
        jnp.stack(input_grads),
        bias_grad,
        first_new,
        second_new,
        bias_new,
        bias_new.astype(jnp.bfloat16),
    )


def solution(mesh):
    placed = (
        P(None, ("dp", "fsdp"), None, None),
        P(None, ("dp", "fsdp"), None, None),
        P(None, ("dp", "fsdp"), None),
        P(None, ("dp", "fsdp"), None),
        P("fsdp", "dp"),
        P("fsdp", "dp"),
        P("fsdp", "dp"),
        P("fsdp", "dp"),
        P(),
        P("fsdp", None, None, None),
        P("fsdp", None, None, None),
        P("fsdp", None, None, None),
        P("fsdp", None, None, None),
        P(),
    )
    return jax.shard_map(
        body,
        mesh=mesh,
        in_specs=placed,
        out_specs=(
            P(None, ("dp", "fsdp"), None, None),
            P(None, ("dp", "fsdp"), None, None),
            P(),
            P("fsdp", None, None, None),
            P("fsdp", None, None, None),
            P(),
            P(),
        ),
        check_vma=False,
    )
```

profile of v0, /device:TPU:0, one launch (start us, length us, event | category | flops | bytes accessed | tf_op | source)
XLA Modules:
  0.0 556.7 jit_solution(11361815699781043629)
XLA Ops:
  7.3 10.6 %all_gather.20 = bf16[1024,192]{0,1:T(8,128)(2,1)} all-gather(bf16[512,192]{0,1:T(8,128)(2,1)} %param.18), channel_id=1, replica_groups=mesh['dp'=16,'fsdp'=2] {'fsdp'}, dimensions={0}, use_global_device_ids=true | all-gather | bytes 589824 | tf_op jit(solution)/shard_map/all_gather | solution.py:27
  23.3 9.0 %all_gather.24 = bf16[1024,256]{1,0:T(8,128)(2,1)} all-gather(bf16[512,256]{1,0:T(8,128)(2,1)} %param.20), channel_id=1, replica_groups=mesh['dp'=16,'fsdp'=2] {'fsdp'}, dimensions={0}, use_global_device_ids=true | all-gather | bytes 786432 | tf_op jit(solution)/shard_map/all_gather | solution.py:38
  32.3 7.4 %all_gather.26 = bf16[4096,64]{0,1:T(8,128)(2,1)} all-gather(bf16[2048,64]{0,1:T(8,128)(2,1)} %param.21), channel_id=1, replica_groups=mesh['dp'=16,'fsdp'=2] {'fsdp'}, dimensions={0}, use_global_device_ids=true | all-gather | bytes 786432 | tf_op jit(solution)/shard_map/all_gather | solution.py:39
  45.2 35.0 %all-gather.6.cloned.1.call-done = bf16[1024,3072]{0,1:T(8,128)(2,1)} async-done(((bf16[1024,192]{0,1:T(8,128)(2,1)}), bf16[1024,3072]{0,1:T(8,128)(2,1)}) %all-gather.6.cloned.1.call-update) | async-done | bytes 6291472 | tf_op jit(solution)/shard_map/all_gather | solution.py:31
  80.2 6.6 %add_convert_fusion = bf16[512,3072]{1,0:T(8,128)(2,1)S(1)} fusion(bf16[1024,3072]{0,1:T(8,128)(2,1)} %all-gather.6.cloned.1.call-done, f32[3072]{0:T(1024)S(1)} %pad_maximum_fusion.2, bf16[2,1,512,1024]{3,2,1,0:T(8,128)(2,1)} %param.14), kind=kOutput, calls=%fused_computation.46 | convolution fusion | flops 3224371200 | bytes 10498048 | tf_op jit(solution)/shard_map/dot_general | solution.py:174
  89.6 8.3 %add_convert_fusion.1 = bf16[512,3072]{1,0:T(8,128)(2,1)} fusion(bf16[1024,3072]{0,1:T(8,128)(2,1)} %all-gather.6.cloned.1.call-done, f32[3072]{0:T(1024)S(1)} %pad_maximum_fusion.2, bf16[2,1,512,1024]{3,2,1,0:T(8,128)(2,1)} %param.14), kind=kOutput, calls=%fused_computation.47 | convolution fusion | flops 3224371200 | bytes 10498048 | tf_op jit(solution)/shard_map/dot_general | solution.py:174
  101.3 11.1 %fusion.144 = (f32[16,512]{1,0:T(8,128)S(1)}, f32[16,512,512]{1,2,0:T(8,128)}) fusion(bf16[1,512,3,16,64]{1,4,3,2,0:T(8,128)(2,1)} %bitcast.232, pred[512,512]{0,1:T(8,128)(4,1)} %get-tuple-element.233), kind=kOutput, calls=%fused_computation.265 | convolution fusion | flops 549445632 | bytes 19169280 | tf_op jit(solution)/shard_map/while/body/eval_jaxpr/qhd,khd->hqk/dot_general | solution.py:121
  112.4 8.4 %fusion.1 = f32[16,512]{1,0:T(8,128)S(1)} fusion(f32[16,512,512]{1,2,0:T(8,128)} %get-tuple-element.217, f32[16,512]{1,0:T(8,128)S(1)} %get-tuple-element.216), kind=kLoop, calls=%fused_computation.13 | loop fusion | flops 8380416 | bytes 16842752 | tf_op jit(solution)/shard_map/while/body/eval_jaxpr/reduce_sum | solution.py:132
  121.4 10.1 %fusion.56 = bf16[16,64,512]{2,1,0:T(8,128)(2,1)} fusion(f32[16,512,512]{1,2,0:T(8,128)} %get-tuple-element.217, f32[16,512]{1,0:T(8,128)S(1)} %fusion.1, f32[16,512]{1,0:T(8,128)S(1)} %get-tuple-element.216, bf16[1,512,3,16,64]{1,4,3,2,0:T(8,128)(2,1)} %bitcast.233), kind=kOutput, calls=%fused_computation.118 | convolution fusion | flops 549978112 | bytes 18939904 | tf_op jit(solution)/shard_map/while/body/eval_jaxpr/hqk,khd->qhd/dot_general | solution.py:134
  136.9 7.7 %fusion.141 = (f32[16,512]{1,0:T(8,128)S(1)}, f32[16,512,512]{1,2,0:T(8,128)}) fusion(bf16[1,512,3,16,64]{1,4,3,2,0:T(8,128)(2,1)S(1)} %bitcast.227, pred[512,512]{0,1:T(8,128)(4,1)S(1)} %get-tuple-element.234), kind=kOutput, calls=%fused_computation.262 | convolution fusion | flops 549445632 | bytes 19169280 | tf_op jit(solution)/shard_map/while/body/eval_jaxpr/qhd,khd->hqk/dot_general | solution.py:121
  144.6 8.3 %fusion = f32[16,512]{1,0:T(8,128)S(1)} fusion(f32[16,512,512]{1,2,0:T(8,128)} %get-tuple-element.211, f32[16,512]{1,0:T(8,128)S(1)} %get-tuple-element.210), kind=kLoop, calls=%fused_computation.12 | loop fusion | flops 8380416 | bytes 16842752 | tf_op jit(solution)/shard_map/while/body/eval_jaxpr/reduce_sum | solution.py:132
  152.9 7.7 %fusion.57 = bf16[16,64,512]{2,1,0:T(8,128)(2,1)S(1)} fusion(f32[16,512,512]{1,2,0:T(8,128)} %get-tuple-element.211, f32[16,512]{1,0:T(8,128)S(1)} %fusion, f32[16,512]{1,0:T(8,128)S(1)} %get-tuple-element.210, bf16[1,512,3,16,64]{1,4,3,2,0:T(8,128)(2,1)S(1)} %bitcast.228), kind=kOutput, calls=%fused_computation.119 | convolution fusion | flops 549978112 | bytes 18939904 | tf_op jit(solution)/shard_map/while/body/eval_jaxpr/hqk,khd->qhd/dot_general | solution.py:134
  163.9 37.6 %all-gather.10.cloned.1.call-done = bf16[1024,4096]{1,0:T(8,128)(2,1)} async-done(((bf16[1024,256]{1,0:T(8,128)(2,1)}), bf16[1024,4096]{1,0:T(8,128)(2,1)}) %all-gather.10.cloned.1.call-update) | async-done | bytes 8388624 | tf_op jit(solution)/shard_map/all_gather | solution.py:42
  201.5 10.3 %fusion.62 = f32[512,4096]{1,0:T(8,128)} fusion(bf16[1024,4096]{1,0:T(8,128)(2,1)} %all-gather.10.cloned.1.call-done, f32[512,1024]{1,0:T(8,128)S(1)} %copy-done.11, f32[512]{0:T(512)S(1)} %add_rsqrt_fusion.1, f32[512]{0:T(512)S(1)} %broadcast_multiply_fusion.11, f32[1024]{0:T(1024)S(1)} %copy-done.39, f32[1024]{0:T(1024)S(1)} %get-tuple-element.195), kind=kOutput, calls=%fused_computation.129 | convolution fusion | flops 4297588736 | bytes 18886656 | tf_op jit(solution)/shard_map/dot_general | solution.py:186
  211.8 64.8 %all-gather.12.cloned.1.call-done = bf16[4096,1024]{0,1:T(8,128)(2,1)} async-done(((bf16[4096,64]{0,1:T(8,128)(2,1)}), bf16[4096,1024]{0,1:T(8,128)(2,1)}) %all-gather.12.cloned.1.call-update) | async-done | bytes 8388624 | tf_op jit(solution)/shard_map/all_gather | solution.py:43
  276.6 10.0 %fusion.146 = (f32[512]{0:T(512)S(1)}, f32[512,1024]{1,0:T(8,128)S(1)}) fusion(f32[1024]{0:T(1024)S(1)} %copy-done.38, bf16[4096,1024]{0,1:T(8,128)(2,1)} %all-gather.12.cloned.1.call-done, f32[512,4096]{1,0:T(8,128)} %fusion.62, f32[4096]{0:T(1024)S(1)} %copy-done.34, f32[1024]{0:T(1024)S(1)} %copy-done.39, f32[1024]{0:T(1024)S(1)} %get-tuple-element.195, ...), kind=kOutput, calls=%fused_computation.267 | convolution fusion | flops 4311219712 | bytes 21006336 | tf_op jit(solution)/shard_map/dot_general | solution.py:188
  287.0 10.5 %fusion.64 = f32[512,4096]{1,0:T(8,128)} fusion(bf16[1024,4096]{1,0:T(8,128)(2,1)} %all-gather.10.cloned.1.call-done, f32[512,1024]{1,0:T(8,128)S(1)} %copy-done.21, f32[1024]{0:T(1024)S(1)} %copy-done.39, f32[1024]{0:T(1024)S(1)} %get-tuple-element.195, f32[512]{0:T(512)S(1)} %add_rsqrt_fusion.3, f32[512]{0:T(512)S(1)} %broadcast_multiply_fusion.13), kind=kOutput, calls=%fused_computation.130 | convolution fusion | flops 4297588736 | bytes 18886656 | tf_op jit(solution)/shard_map/dot_general | solution.py:186
  297.4 9.9 %fusion.143 = (f32[512]{0:T(512)S(1)}, f32[512,1024]{1,0:T(8,128)S(1)}) fusion(f32[1024]{0:T(1024)S(1)} %copy-done.38, bf16[4096,1024]{0,1:T(8,128)(2,1)} %all-gather.12.cloned.1.call-done, f32[512,4096]{1,0:T(8,128)} %fusion.64, f32[4096]{0:T(1024)S(1)} %copy-done.34, f32[1024]{0:T(1024)S(1)} %copy-done.39, f32[1024]{0:T(1024)S(1)} %get-tuple-element.195, ...), kind=kOutput, calls=%fused_computation.264 | convolution fusion | flops 4311219712 | bytes 21006336 | tf_op jit(solution)/shard_map/dot_general | solution.py:188
  313.8 9.4 %convert_reduce_fusion.1 = (f32[4096]{0:T(1024)S(1)}, bf16[512,4096]{1,0:T(8,128)(2,1)S(1)}) fusion(f32[512,4096]{1,0:T(8,128)} %fusion.64, f32[4096]{0:T(1024)S(1)} %copy-done.34, bf16[4096,1024]{0,1:T(8,128)(2,1)S(1)} %bitcast.247, f32[512,1024]{1,0:T(8,128)S(1)} %get-tuple-element.180), kind=kOutput, calls=%fused_computation.33 | convolution fusion | flops 4322750464 | bytes 23101440 | tf_op jit(solution)/shard_map/rd,fd->rf/dot_general | solution.py:216
  323.2 9.8 %multiply_reduce_fusion.3 = (f32[1024]{0:T(1024)S(1)}, f32[512]{0:T(512)S(1)}, f32[512]{0:T(512)S(1)}, f32[1024]{0:T(1024)S(1)}, f32[512,1024]{1,0:T(8,128)}) fusion(f32[512,1024]{1,0:T(8,128)S(1)} %copy-done.21, f32[512]{0:T(512)S(1)} %add_rsqrt_fusion.3, f32[512]{0:T(512)S(1)} %broadcast_multiply_fusion.13, f32[1024]{0:T(1024)S(1)} %get-tuple-element.195, ...), kind=kOutput, calls=%fused_computation.81 | convolution fusion | flops 4300207104 | bytes 18894848 | tf_op jit(solution)/shard_map/rf,df->rd/dot_general | solution.py:219
  333.0 12.3 %convert_reduce_fusion = (f32[4096]{0:T(1024)S(1)}, bf16[512,4096]{1,0:T(8,128)(2,1)}) fusion(f32[512,4096]{1,0:T(8,128)} %fusion.62, f32[4096]{0:T(1024)S(1)} %copy-done.34, bf16[4096,1024]{0,1:T(8,128)(2,1)} %all-gather.12.cloned.1.call-done, f32[512,1024]{1,0:T(8,128)S(1)} %get-tuple-element.156), kind=kOutput, calls=%fused_computation.32 | convolution fusion | flops 4322750464 | bytes 23101440 | tf_op jit(solution)/shard_map/rd,fd->rf/dot_general | solution.py:216
  345.3 10.8 %convert_reduce_fusion.9 = (f32[1024]{0:T(1024)S(1)}, f32[512,1024]{1,0:T(8,128)}, f32[1024]{0:T(1024)S(1)}, f32[512]{0:T(512)S(1)}, f32[512]{0:T(512)S(1)}, /*index=5*/f32[1024]{0:T(1024)S(1)}, f32[512,1024]{1,0:T(8,128)S(1)}) fusion(f32[512]{0:T(512)S(1)} %broadcast_multiply_fusion.6, f32[512,1024]{1,0:T(8,128)S(1)} %copy-done.21, ...), kind=kOutput, calls=%fused_computation.83 | convolution fusion | flops 4305448960 | bytes 25198592 | tf_op jit(solution)/shard_map/rf,df->rd/dot_general | solution.py:219
  360.0 11.6 %multiply_reduce_fusion = (f32[16,512]{1,0:T(8,128)S(1)}, f32[16,512,512]{1,2,0:T(8,128)}) fusion(f32[16,512,512]{1,2,0:T(8,128)} %get-tuple-element.217, f32[16,512]{1,0:T(8,128)S(1)} %log_add_fusion, bf16[512,16,64]{0,2,1:T(8,128)(2,1)S(1)} %bitcast.237, bf16[1,512,3,16,64]{1,4,3,2,0:T(8,128)(2,1)} %bitcast.234), kind=kOutput, calls=%fused_computation.1 | convolution fusion | flops 549445632 | bytes 35717120 | tf_op jit(solution)/shard_map/while/body/eval_jaxpr/qhd,khd->hqk/dot_general | solution.py:143
  371.6 11.8 %multiply_convert_fusion = bf16[16,512,512]{1,2,0:T(8,128)(2,1)S(1)} fusion(f32[16,512,512]{1,2,0:T(8,128)} %get-tuple-element.225, f32[16,512,512]{1,2,0:T(8,128)} %get-tuple-element.217, f32[16,512]{1,0:T(8,128)S(1)} %get-tuple-element.224, f32[16,512]{1,0:T(8,128)S(1)} %log_add_fusion), kind=kLoop, calls=%fused_computation | loop fusion | flops 16777216 | bytes 42008576 | tf_op jit(solution)/shard_map/while/body/eval_jaxpr/convert_element_type | solution.py:145
  390.2 7.2 %multiply_bitcast_fusion = bf16[512,1,16,64]{0,3,2,1:T(8,128)(2,1)} fusion(bf16[16,512,512]{1,2,0:T(8,128)(2,1)} %copy-done.1, bf16[1,512,3,16,64]{1,4,3,2,0:T(8,128)(2,1)S(1)} %bitcast.236), kind=kOutput, calls=%fused_computation.85 | convolution fusion | flops 537919488 | bytes 10485760 | tf_op jit(solution)/shard_map/while/body/eval_jaxpr/hqk,qhd->khd/dot_general | solution.py:149
  406.6 11.7 %multiply_reduce_fusion.1 = (f32[16,512]{1,0:T(8,128)S(1)}, f32[16,512,512]{1,2,0:T(8,128)}) fusion(f32[16,512,512]{1,2,0:T(8,128)} %get-tuple-element.211, f32[16,512]{1,0:T(8,128)S(1)} %log_add_fusion.1, bf16[512,16,64]{0,2,1:T(8,128)(2,1)S(1)} %bitcast.239, bf16[1,512,3,16,64]{1,4,3,2,0:T(8,128)(2,1)} %bitcast.229), kind=kOutput, calls=%fused_computation.4 | convolution fusion | flops 549445632 | bytes 35717120 | tf_op jit(solution)/shard_map/while/body/eval_jaxpr/qhd,khd->hqk/dot_general | solution.py:143
  418.3 11.8 %multiply_convert_fusion.1 = bf16[16,512,512]{1,2,0:T(8,128)(2,1)S(1)} fusion(f32[16,512,512]{1,2,0:T(8,128)} %get-tuple-element.227, f32[16,512,512]{1,2,0:T(8,128)} %get-tuple-element.211, f32[16,512]{1,0:T(8,128)S(1)} %get-tuple-element.226, f32[16,512]{1,0:T(8,128)S(1)} %log_add_fusion.1), kind=kLoop, calls=%fused_computation.3 | loop fusion | flops 16777216 | bytes 42008576 | tf_op jit(solution)/shard_map/while/body/eval_jaxpr/convert_element_type | solution.py:145
  436.8 7.2 %multiply_bitcast_fusion.2 = bf16[512,1,16,64]{0,3,2,1:T(8,128)(2,1)} fusion(bf16[16,512,512]{1,2,0:T(8,128)(2,1)} %copy-done.2, bf16[1,512,3,16,64]{1,4,3,2,0:T(8,128)(2,1)S(1)} %bitcast.231), kind=kOutput, calls=%fused_computation.90 | convolution fusion | flops 537919488 | bytes 10485760 | tf_op jit(solution)/shard_map/while/body/eval_jaxpr/hqk,qhd->khd/dot_general | solution.py:149
  456.5 7.9 %fusion.58 = bf16[1,1,512,1024]{3,2,1,0:T(8,128)(2,1)S(1)} fusion(f32[512,1024]{1,0:T(8,128)} %get-tuple-element.164, bf16[512,3072]{0,1:T(8,128)(2,1)} %bitcast.242, bf16[1024,3072]{0,1:T(8,128)(2,1)} %all-gather.6.cloned.1.call-done), kind=kOutput, calls=%fused_computation.122 | convolution fusion | flops 3222274048 | bytes 12582912 | tf_op jit(solution)/shard_map/re,de->rd/dot_general | solution.py:245
  464.4 6.2 %fusion.59 = bf16[1,1,512,1024]{3,2,1,0:T(8,128)(2,1)S(1)} fusion(f32[512,1024]{1,0:T(8,128)S(1)} %copy-done.19, bf16[512,3072]{0,1:T(8,128)(2,1)S(1)} %bitcast.241, bf16[1024,3072]{0,1:T(8,128)(2,1)} %all-gather.6.cloned.1.call-done), kind=kOutput, calls=%fused_computation.123 | convolution fusion | flops 3222274048 | bytes 12582912 | tf_op jit(solution)/shard_map/re,de->rd/dot_general | solution.py:245
  474.5 59.7 %psum.8 = bf16[1,6,32,32]{3,2,1,0:T(8,128)(2,1)S(1)} all-reduce(bf16[1,6,32,32]{3,2,1,0:T(8,128)(2,1)} %reduce-scatter.2.cloned.1.call-done), channel_id=1, replica_groups=mesh['dp'=16,'fsdp'=2] {'dp'}, use_global_device_ids=true, to_apply=%region_39.40 | all-reduce | flops 6144 | bytes 24576 | tf_op jit(solution)/shard_map/psum | solution.py:352
  536.0 6.2 %all-gather = f32[12,32,32]{2,1,0:T(8,128)S(1)} all-gather(f32[6,32,32]{2,1,0:T(8,128)S(1)} %fusion.61), channel_id=2, replica_groups=mesh['dp'=16,'fsdp'=2] {'fsdp'}, dimensions={0}, use_global_device_ids=true | all-gather | bytes 73728 | tf_op jit(solution)/shard_map/all_gather | solution.py:369
  (229 shorter events, 85.0 us)
Async XLA Ops:
  7.2 527.3 %copy-start = (f32[1,6,32,32]{3,2,1,0:T(8,128)S(1)}, f32[1,6,32,32]{3,2,1,0:T(8,128)}, u32[]{:S(2)}) copy-start(f32[1,6,32,32]{3,2,1,0:T(8,128)} %param.26) | copy-start | bytes 73732
  7.2 32.6 %copy-start.24 = (f32[12288]{0:T(1024)S(1)}, f32[12288]{0:T(1024)}, u32[]{:S(2)}) copy-start(f32[12288]{0:T(1024)} %param.22) | copy-start | bytes 147460
  7.2 33.3 %copy-start.47 = (s32[12]{0:T(128)S(1)}, s32[12]{0:T(128)}, u32[]{:S(2)}) copy-start(s32[12]{0:T(128)} %param.27) | copy-start | bytes 148
  7.2 34.8 %copy-start.42 = (s32[2,1,512]{2,1,0:T(1,128)S(1)}, s32[2,1,512]{2,1,0:T(1,128)}, u32[]{:S(2)}) copy-start(s32[2,1,512]{2,1,0:T(1,128)} %param.17) | copy-start | bytes 12292
  7.2 34.8 %copy-start.6 = (bf16[2,1,512,1024]{3,2,1,0:T(8,128)(2,1)S(1)}, bf16[2,1,512,1024]{3,2,1,0:T(8,128)(2,1)}, u32[]{:S(2)}) copy-start(bf16[2,1,512,1024]{3,2,1,0:T(8,128)(2,1)} %param.15) | copy-start | bytes 6291460
  7.2 35.8 %copy-start.43 = (s32[2,1,512]{2,1,0:T(1,128)S(1)}, s32[2,1,512]{2,1,0:T(1,128)}, u32[]{:S(2)}) copy-start(s32[2,1,512]{2,1,0:T(1,128)} %param.16) | copy-start | bytes 12292
  7.2 73.0 %all-gather.6.cloned.1.call-start = ((), (), s32[]{:S(2)}) async-start(), calls=%async_computation.1 | async-start | bytes 6684672 | tf_op jit(solution)/shard_map/all_gather | solution.py:31
  17.9 113.6 %all-gather.8.cloned.1.call-start = ((), (), s32[]{:S(2)}) async-start(), calls=%async_computation.2 | async-start | bytes 2228224 | tf_op jit(solution)/shard_map/all_gather | solution.py:32
  23.2 178.2 %all-gather.10.cloned.1.call-start = ((), (), s32[]{:S(2)}) async-start(), calls=%async_computation.3 | async-start | bytes 8912896 | tf_op jit(solution)/shard_map/all_gather | solution.py:42
  32.2 244.3 %all-gather.12.cloned.1.call-start = ((), (), s32[]{:S(2)}) async-start(), calls=%async_computation.4 | async-start | bytes 8912896 | tf_op jit(solution)/shard_map/all_gather | solution.py:43
  39.7 434.8 %reduce-scatter.2.cloned.1.call-start = ((), (), s32[]{:S(2)}) async-start(), calls=%async_computation.5 | async-start | bytes 147456 | tf_op jit(solution)/shard_map/reduce_scatter | solution.py:353
  101.3 51.6 %copy-start.3 = (bf16[512,3072]{0,1:T(8,128)(2,1)}, bf16[512,3072]{0,1:T(8,128)(2,1)S(1)}, u32[]{:S(2)}) copy-start(bf16[512,3072]{0,1:T(8,128)(2,1)S(1)} %copy.111) | copy-start | bytes 9437188
  160.7 40.8 %copy-start.11 = (f32[512,1024]{1,0:T(8,128)S(1)}, f32[512,1024]{1,0:T(8,128)}, u32[]{:S(2)}) copy-start(f32[512,1024]{1,0:T(8,128)} %copy-done.10) | copy-start | bytes 6291460
  160.7 40.8 %copy-start.39 = (f32[1024]{0:T(1024)S(1)}, f32[1024]{0:T(1024)}, u32[]{:S(2)}) copy-start(f32[1024]{0:T(1024)} %get-tuple-element.194) | copy-start | bytes 12292
  201.5 75.1 %copy-start.34 = (f32[4096]{0:T(1024)S(1)}, f32[4096]{0:T(1024)}, u32[]{:S(2)}) copy-start(f32[4096]{0:T(1024)} %slice.153) | copy-start | bytes 49156
  201.5 75.1 %copy-start.38 = (f32[1024]{0:T(1024)S(1)}, f32[1024]{0:T(1024)}, u32[]{:S(2)}) copy-start(f32[1024]{0:T(1024)} %get-tuple-element.193) | copy-start | bytes 12292
  276.6 10.4 %copy-start.21 = (f32[512,1024]{1,0:T(8,128)S(1)}, f32[512,1024]{1,0:T(8,128)}, u32[]{:S(2)}) copy-start(f32[512,1024]{1,0:T(8,128)} %copy-done.20) | copy-start | bytes 6291460
  360.0 11.6 %copy-start.8 = (bf16[512,1024]{0,1:T(8,128)(2,1)}, bf16[512,1024]{0,1:T(8,128)(2,1)S(1)}, u32[]{:S(2)}) copy-start(bf16[512,1024]{0,1:T(8,128)(2,1)S(1)} %copy.119) | copy-start | bytes 3145732
  371.6 16.1 %copy-start.5 = (bf16[512,3072]{0,1:T(8,128)(2,1)S(1)}, bf16[512,3072]{0,1:T(8,128)(2,1)}, u32[]{:S(2)}) copy-start(bf16[512,3072]{0,1:T(8,128)(2,1)} %copy.113) | copy-start | bytes 9437188
  371.6 25.8 %slice-start = ((s8[16777216]{0:T(1024)(128)(4,1)}), s8[4194304]{0:T(1024)(128)(4,1)S(1)}, s32[]{:S(2)}) async-start(s8[16777216]{0:T(1024)(128)(4,1)} %bitcast.223), calls=%async_computation.6 | async-start | bytes 8388608
  371.6 25.8 %slice-start.1 = ((s8[16777216]{0:T(1024)(128)(4,1)}), s8[4194304]{0:T(1024)(128)(4,1)S(1)}, s32[]{:S(2)}) async-start(s8[16777216]{0:T(1024)(128)(4,1)} %bitcast.223), calls=%async_computation.7 | async-start | bytes 8388608
  371.6 25.8 %slice-start.2 = ((s8[16777216]{0:T(1024)(128)(4,1)}), s8[4194304]{0:T(1024)(128)(4,1)S(1)}, s32[]{:S(2)}) async-start(s8[16777216]{0:T(1024)(128)(4,1)} %bitcast.223), calls=%async_computation.8 | async-start | bytes 8388608
  406.6 11.7 %copy-start.9 = (bf16[512,1024]{0,1:T(8,128)(2,1)}, bf16[512,1024]{0,1:T(8,128)(2,1)S(1)}, u32[]{:S(2)}) copy-start(bf16[512,1024]{0,1:T(8,128)(2,1)S(1)} %copy.115) | copy-start | bytes 3145732
  418.3 16.1 %copy-start.4 = (bf16[512,3072]{0,1:T(8,128)(2,1)S(1)}, bf16[512,3072]{0,1:T(8,128)(2,1)}, u32[]{:S(2)}) copy-start(bf16[512,3072]{0,1:T(8,128)(2,1)} %copy-done.3) | copy-start | bytes 9437188
  418.3 25.8 %slice-start.4 = ((s8[16777216]{0:T(1024)(128)(4,1)}), s8[4194304]{0:T(1024)(128)(4,1)S(1)}, s32[]{:S(2)}) async-start(s8[16777216]{0:T(1024)(128)(4,1)} %bitcast.225), calls=%async_computation.10 | async-start | bytes 8388608
  418.3 25.8 %slice-start.5 = ((s8[16777216]{0:T(1024)(128)(4,1)}), s8[4194304]{0:T(1024)(128)(4,1)S(1)}, s32[]{:S(2)}) async-start(s8[16777216]{0:T(1024)(128)(4,1)} %bitcast.225), calls=%async_computation.11 | async-start | bytes 8388608
  418.3 25.8 %slice-start.6 = ((s8[16777216]{0:T(1024)(128)(4,1)}), s8[4194304]{0:T(1024)(128)(4,1)S(1)}, s32[]{:S(2)}) async-start(s8[16777216]{0:T(1024)(128)(4,1)} %bitcast.225), calls=%async_computation.12 | async-start | bytes 8388608
  472.2 62.0 %copy-start.29 = (f32[1,6,32,32]{3,2,1,0:T(8,128)S(1)}, f32[1,6,32,32]{3,2,1,0:T(8,128)}, u32[]{:S(2)}) copy-start(f32[1,6,32,32]{3,2,1,0:T(8,128)} %param.25) | copy-start | bytes 73732
  472.2 62.2 %copy-start.27 = (f32[1,6,32,32]{3,2,1,0:T(8,128)S(1)}, f32[1,6,32,32]{3,2,1,0:T(8,128)}, u32[]{:S(2)}) copy-start(f32[1,6,32,32]{3,2,1,0:T(8,128)} %param.24) | copy-start | bytes 73732
  472.2 62.3 %copy-start.28 = (f32[1,6,32,32]{3,2,1,0:T(8,128)S(1)}, f32[1,6,32,32]{3,2,1,0:T(8,128)}, u32[]{:S(2)}) copy-start(f32[1,6,32,32]{3,2,1,0:T(8,128)} %param.23) | copy-start | bytes 73732
  472.2 62.3 %copy-start.37 = (f32[6]{0:T(128)S(1)}, f32[6]{0:T(128)}, u32[]{:S(2)}) copy-start(f32[6]{0:T(128)} %convert_reduce_fusion.11) | copy-start | bytes 76
  472.2 63.5 %copy-start.22 = (f32[6,32,32]{2,0,1:T(8,128)S(1)}, f32[6,32,32]{2,0,1:T(8,128)}, u32[]{:S(2)}) copy-start(f32[6,32,32]{2,0,1:T(8,128)} %fusion.89) | copy-start | bytes 73732
  (31 other events, 131.1 us)
Sparse Core Ops, SparseCore 0:
  18.0 62.1 all-gather.5
  82.4 39.9 all-gather.7
  124.6 76.8 all-gather.9
  203.5 73.0 all-gather.11
  456.6 8.2 reduce-scatter.1
where the time goes:
time: 564 us; the launch traced here: 557 us
  matrix products  215 us (38%)
  waiting for transfers between devices  137 us (24%)
  blocking collectives  103 us (18%)
  other arithmetic  59.7 us (11%)
  local copies, waits for them, and re-layouts  25.9 us (5%)
  between operations  15.1 us (3%)
    all_gather x1, waiting for transfers between devices, gather_feed(): lax.all_gather(down_rows, 'dp', axis=1, tiled=True)  64.8 us
    psum x1, blocking collectives, body(): summed = lax.psum(grad_slots.astype(jnp.bfloat16), 'dp')  59.7 us
    all_gather x1, waiting for transfers between devices, gather_feed(): lax.all_gather(in_rows, 'dp', axis=1, tiled=True)  37.6 us
    all_gather x1, waiting for transfers between devices, gather_attention(): lax.all_gather(qkv_rows, 'dp', axis=1, tiled=True)  35 us
    convert_element_type x2, other arithmetic, attend_backward(): grad_scores = (attn_probs * (grad_probs - row_inner)).astype(jnp.bfloat16)  23.7 us
    dot_general x2, matrix products, attend_backward(): jnp.einsum('qhd,khd->hqk', grad_ctx, values, preferred_element_type=jnp.f...  23.3 us
    dot_general x2, matrix products, layer_backward(): jnp.einsum('rd,fd->rf', grad_feed, down_weight, preferred_element_type=jn...  21.7 us
    dot_general x2, matrix products, layer_forward(): jnp.dot(hidden_low, in_weight, preferred_element_type=jnp.float32) + up_bias  20.8 us
  transfers between devices with their start and end apart: 5, of which 3 were waited for; matrix products, arithmetic and copies ran while one was open for 20% of the time, Pallas kernels for 0%

commit v1 on v0

--- a/solution.py
+++ b/solution.py
@@ -1,8 +1,11 @@
+import functools
 import math
 
 import jax
 import jax.numpy as jnp
 from jax import lax
+from jax.experimental import pallas as pl
+from jax.experimental.pallas import tpu as pltpu
 from jax.sharding import PartitionSpec as P
 
 D = 1024
@@ -22,48 +25,177 @@
 step_rate = 0.4
 
 
-def gather_attention(qkv_shard, out_shard):
-    qkv_rows, out_rows = (
-        lax.all_gather(qkv_shard, "fsdp", axis=0, tiled=True),
-        lax.all_gather(out_shard, "fsdp", axis=0, tiled=True),
-    )
-    return (
-        lax.all_gather(qkv_rows, "dp", axis=1, tiled=True),
-        lax.all_gather(out_rows, "dp", axis=1, tiled=True),
-    )
-
-
-def gather_feed(in_shard, down_shard):
-    in_rows, down_rows = (
-        lax.all_gather(in_shard, "fsdp", axis=0, tiled=True),
-        lax.all_gather(down_shard, "fsdp", axis=0, tiled=True),
-    )
-    return (
-        lax.all_gather(in_rows, "dp", axis=1, tiled=True),
-        lax.all_gather(down_rows, "dp", axis=1, tiled=True),
-    )
-
-
-def gather_attention_back(qkv_shard, out_shard):
-    qkv_rows, out_rows = (
-        lax.all_gather(qkv_shard, "fsdp", axis=0, tiled=True),
-        lax.all_gather(out_shard, "fsdp", axis=0, tiled=True),
-    )
-    return (
-        lax.all_gather(qkv_rows, "dp", axis=1, tiled=True),
-        lax.all_gather(out_rows, "dp", axis=1, tiled=True),
-    )
-
-
-def gather_feed_back(in_shard, down_shard):
-    in_rows, down_rows = (
-        lax.all_gather(in_shard, "fsdp", axis=0, tiled=True),
-        lax.all_gather(down_shard, "fsdp", axis=0, tiled=True),
-    )
-    return (
-        lax.all_gather(in_rows, "dp", axis=1, tiled=True),
-        lax.all_gather(down_rows, "dp", axis=1, tiled=True),
-    )
+MESH=pl.DeviceIdType.MESH
+NZ=4
+
+def split_rows(R,L,a,b,unit=16):
+    out=[];r=0
+    for kind,n in (("A1",a),("A2",a),("B1",b),("B2",b)):
+        if n: out.append((kind,r,n,0,L)); r+=n
+    assert r==R,(r,R)
+    return out
+def split_lanes(R,L,a,b):
+    out=[];l=0
+    for kind,n in (("A1",a),("A2",a),("B1",b),("B2",b)):
+        if n: out.append((kind,0,R,l,n)); l+=n
+    assert l==L
+    return out
+
+def children(kind,dz,rx,ry):
+    out=[]
+    if kind[0]=="A":
+        if rx==0 and ry==0:
+            if dz>=0: out.append(("zp",(dz+1,0,0)))
+            if dz<=0: out.append(("zm",(dz-1,0,0)))
+            out.append(("x",(dz,1,0))); out.append(("y",(dz,0,1)))
+        if kind=="A1" and (rx,ry)==(1,0): out.append(("y",(dz,1,1)))
+        if kind=="A2" and (rx,ry)==(0,1): out.append(("x",(dz,1,1)))
+    else:
+        if dz==0:
+            if (rx,ry)==(0,0): out += [("x",(0,1,0)),("y",(0,0,1))]
+            if kind=="B1" and (rx,ry)==(1,0): out.append(("y",(0,1,1)))
+            if kind=="B2" and (rx,ry)==(0,1): out.append(("x",(0,1,1)))
+        if dz>=0: out.append(("zp",(dz+1,rx,ry)))
+        if dz<=0: out.append(("zm",(dz-1,rx,ry)))
+    return [(d,c) for d,c in out if abs(c[0])<=NZ-1]
+
+def rel_index(dz,rx,ry): return (dz+3)*4+rx*2+ry
+EVENTS=[(dz,rx,ry) for dz in range(-3,4) for rx in (0,1) for ry in (0,1) if (dz,rx,ry)!=(0,0,0)]
+EVENTS.sort(key=lambda e:(abs(e[0])+e[1]+e[2], e[1]+e[2], -e[0]))
+
+def region(total, N, K):
+    for lanes in range(128,K+1,128):
+        if total%lanes==0:
+            rows=total//lanes
+            if rows%16==0 and rows<=N: return rows,lanes
+    raise ValueError((total,N,K))
+
+class Gather:
+    def __init__(self, mats, shards, fulls, local_sem, send_sem, recv_sem, sib_sem):
+        self.mats=mats; self.sh=shards; self.full=fulls
+        self.lsem,self.ssem,self.rsem,self.bsem=local_sem,send_sem,recv_sem,sib_sem
+        dp=lax.axis_index("dp"); x=lax.axis_index("fsdp")
+        self.dp,self.x=dp,x
+        self.z=dp//4; self.y=(dp//2)%2; self.c=dp%2
+        self.dev={"x":(dp,1-x),"y":(self.z*4+(1-self.y)*2+self.c,x),"zp":(dp+4,x),"zm":(dp-4,x),"s":(self.z*4+self.y*2+1-self.c,x)}
+    def barrier(self):
+        bar=pltpu.get_barrier_semaphore()
+        for d in ("x","y","s"):
+            pl.semaphore_signal(bar,inc=1,device_id=self.dev[d],device_id_type=MESH)
+        @pl.when(self.z<NZ-1)
+        def _(): pl.semaphore_signal(bar,inc=1,device_id=self.dev["zp"],device_id_type=MESH)
+        @pl.when(self.z>0)
+        def _(): pl.semaphore_signal(bar,inc=1,device_id=self.dev["zm"],device_id_type=MESH)
+        inner=(self.z>0)&(self.z<NZ-1)
+        @pl.when(inner)
+        def _(): pl.semaphore_wait(bar,5)
+        @pl.when(jnp.logical_not(inner))
+        def _(): pl.semaphore_wait(bar,4)
+    def place(self,m,k,dz,rx,ry):
+        M=self.mats[m]; kind,r0,nr,l0,nl=M["classes"][k]
+        y=self.y if not ry else 1-self.y
+        x=self.x if not rx else 1-self.x
+        src=(self.z-dz)*4+y*2+self.c
+        return self.full[m].at[pl.ds(pl.multiple_of(src*M["R"]+r0,16),nr), pl.ds(pl.multiple_of(x*M["L"]+l0,128),nl)]
+    def forward(self,m,k,rel,src,extra=True):
+        M=self.mats[m]; kind=M["classes"][k][0]
+        dst=self.place(m,k,*rel)
+        for d,ch in children(kind,*rel):
+            def go(d=d,ch=ch):
+                pltpu.make_async_remote_copy(src,dst,self.ssem.at[m,["x","y","zp","zm","s"].index(d)],self.rsem.at[m,k,rel_index(*ch)],
+                    device_id=self.dev[d],device_id_type=MESH).start()
+            if d=="zp": pl.when(self.z<NZ-1)(go)
+            elif d=="zm": pl.when(self.z>0)(go)
+            else: go()
+        pltpu.make_async_remote_copy(src,dst,self.ssem.at[m,4],self.bsem.at[m],device_id=self.dev["s"],device_id_type=MESH).start()
+    def own(self,m):
+        M=self.mats[m]
+        for k,(kind,r0,nr,l0,nl) in enumerate(M["classes"]):
+            self.forward(m,k,(0,0,0),self.sh[m].at[pl.ds(r0,nr),pl.ds(l0,nl)])
+        full=self.full[m].at[pl.ds(pl.multiple_of(self.dp*M["R"],16),M["R"]),pl.ds(pl.multiple_of(self.x*M["L"],128),M["L"])]
+        pltpu.make_async_copy(self.sh[m],full,self.lsem.at[m]).start()
+    def events(self,m):
+        out=[]
+        for rel in EVENTS:
+            for k in range(len(self.mats[m]["classes"])):
+                out.append(functools.partial(self.event,m,k,rel))
+        return out
+    def event(self,m,k,rel):
+        def go():
+            ref=self.place(m,k,*rel)
+            pltpu.make_async_copy(ref,ref,self.rsem.at[m,k,rel_index(*rel)]).wait()
+            self.forward(m,k,rel,ref)
+        dz=rel[0]
+        if dz>0: pl.when(self.z>=dz)(go)
+        elif dz<0: pl.when(self.z<=NZ-1+dz)(go)
+        else: go()
+    def wait_bytes(self,m,total,sem):
+        N,K=self.full[m].shape
+        r,l=region(total,N,K)
+        ref=self.full[m].at[pl.ds(0,r),pl.ds(0,l)]
+        pltpu.make_async_copy(ref,ref,sem).wait()
+    def finish_recv(self,m):
+        M=self.mats[m]
+        own=self.sh[m]
+        pltpu.make_async_copy(own,own,self.lsem.at[m]).wait()
+        N,K=self.full[m].shape
+        self.wait_bytes(m,N*K//2,self.bsem.at[m])
+    def finish_send(self,m):
+        M=self.mats[m]; N,K=self.full[m].shape
+        def total(d,z):
+            t=0
+            for kind,r0,nr,l0,nl in M["classes"]:
+                for rel in [(0,0,0)]+EVENTS:
+                    if not 0<=z-rel[0]<=NZ-1: continue
+                    for dd,ch in children(kind,*rel):
+                        if dd==d and not (d=="zp" and z==NZ-1) and not (d=="zm" and z==0): t+=nr*nl
+            return t
+        for i,d in enumerate(("x","y")):
+            self.wait_bytes(m,total(d,0),self.ssem.at[m,i]); assert total(d,0)==total(d,2)
+        for i,d in ((2,"zp"),(3,"zm")):
+            for z in range(NZ):
+                if total(d,z):
+                    pl.when(self.z==z)(functools.partial(self.wait_bytes,m,total(d,z),self.ssem.at[m,i]))
+        self.wait_bytes(m,N*K//2,self.ssem.at[m,4])
+
+def plain(mats,*refs):
+    n=len(mats)
+    sh=refs[:n]; full=refs[n:2*n]; sems=refs[2*n:]
+    g=Gather(mats,sh,full,*sems)
+    g.barrier()
+    g.own(0)
+    for m in range(n):
+        ev=g.events(m)
+        for i,e in enumerate(ev):
+            if i==len(ev)//2 and m+1<n: g.own(m+1)
+            e()
+    for m in range(n):
+        g.finish_recv(m); g.finish_send(m)
+
+def gather_call(mats,shards,cid):
+    n=len(mats)
+    outs=[jax.ShapeDtypeStruct((s.shape[0]*16,s.shape[1]*2),jnp.bfloat16) for s in shards]
+    return pl.pallas_call(functools.partial(plain,mats),out_shape=outs,
+        in_specs=[pl.BlockSpec(memory_space=pl.ANY)]*n,out_specs=[pl.BlockSpec(memory_space=pl.ANY)]*n,
+        scratch_shapes=[pltpu.SemaphoreType.DMA((n,)),pltpu.SemaphoreType.DMA((n,5)),pltpu.SemaphoreType.DMA((n,4,28)),pltpu.SemaphoreType.DMA((n,))],
+        compiler_params=pltpu.CompilerParams(collective_id=cid,has_side_effects=True,vmem_limit_bytes=60<<20))(*shards)
+
+def matdesc(beta=True):
+    if beta:
+        return [dict(R=192,L=512,classes=split_rows(192,512,80,16)),dict(R=64,L=512,classes=split_rows(64,512,32,0)),
+            dict(R=256,L=512,classes=split_rows(256,512,96,32)),dict(R=64,L=2048,classes=split_lanes(64,2048,768,256))]
+    return [dict(R=192,L=512,classes=split_rows(192,512,96,0)),dict(R=64,L=512,classes=split_rows(64,512,32,0)),
+            dict(R=256,L=512,classes=split_rows(256,512,128,0)),dict(R=64,L=2048,classes=split_lanes(64,2048,1024,0))]
+
+
+def gather_weights(shards):
+    turned = [s.T for s in shards]
+    if (lax.axis_size("dp"), lax.axis_size("fsdp")) == (16, 2):
+        return gather_call(matdesc(), turned, 1)
+    return [
+        lax.all_gather(lax.all_gather(t, "fsdp", axis=1, tiled=True), "dp", axis=0, tiled=True)
+        for t in turned
+    ]
 
 
 def split_biases(bias_vec):
@@ -304,42 +436,20 @@
     basis_right,
     owners,
 ):
-    grad_total = jnp.zeros((biases.shape[0],), jnp.float32)
-    outputs = []
-    input_grads = []
-    for batch_index in range(MB):
-        attn_now = gather_attention(qkv_weight, out_weight)
-        feed_now = gather_feed(in_weight, down_weight)
-        result, first_state = layer_forward(
-            acts[batch_index],
-            seg_ids[batch_index],
-            pad_mask[batch_index],
-            attn_now,
-            feed_now,
-            biases,
-        )
-        outputs.append(result.astype(jnp.bfloat16))
-        attn_back = gather_attention_back(qkv_weight, out_weight)
-        feed_back = gather_feed_back(in_weight, down_weight)
-        result_again, kept_state = layer_forward(
-            acts[batch_index],
-            seg_ids[batch_index],
-            pad_mask[batch_index],
-            attn_back,
-            feed_back,
-            biases,
-        )
-        grad_inputs, bias_part = layer_backward(
-            cotangent[batch_index],
-            kept_state,
-            seg_ids[batch_index],
-            pad_mask[batch_index],
-            attn_back,
-            feed_back,
-            biases,
-        )
-        input_grads.append(grad_inputs)
-        grad_total = grad_total + bias_part
+    full = gather_weights((qkv_weight, out_weight, in_weight, down_weight))
+    attn_now = (full[0].T, full[1].T)
+    feed_now = (full[2].T, full[3].T)
+    slots = acts.shape[0] * acts.shape[1]
+    segs = seg_ids.reshape(slots, SEQ)
+    pads = pad_mask.reshape(slots, SEQ)
+    result, kept_state = layer_forward(
+        acts.reshape(slots, SEQ, D), segs, pads, attn_now, feed_now, biases
+    )
+    grad_inputs, grad_total = layer_backward(
+        cotangent.reshape(slots, SEQ, D), kept_state, segs, pads, attn_now, feed_now, biases
+    )
+    outputs = result.astype(jnp.bfloat16).reshape(acts.shape)
+    input_grads = grad_inputs.reshape(acts.shape)
     block_count = owners.shape[0]
     block_side = moment_first.shape[2]
     slot_table = placement_table(owners, lax.axis_size("fsdp"), moment_first.shape[1])
@@ -375,8 +485,8 @@
         biases.shape[0]
     )
     return (
-        jnp.stack(outputs),
-        jnp.stack(input_grads),
+        outputs,
+        input_grads,
         bias_grad,
         first_new,
         second_new,

time: 564 us -> 533 us (0.945)
  waiting for transfers between devices: 137 us -> 0.03 us
  Pallas kernels: 0 us -> 105 us
  local copies, waits for them, and re-layouts: 25.9 us -> 64.5 us
  blocking collectives: 103 us -> 72.4 us
  matrix products: 215 us -> 198 us
  other arithmetic: 59.7 us -> 68.3 us
    all_gather x4 -> x0, waiting for transfers between devices: 137 us -> none  [the longest x1 64.8 us: gather_feed(): lax.all_gather(down_rows, 'dp', axis=1, tiled=True)]
    pallas_call x0 -> x1, Pallas kernels: none -> 105 us  [gather_call(): pl.pallas_call(functools.partial(plain, mats), out_shape=outs, in_specs=[...]
    all_gather x4 -> x0, blocking collectives: 32.2 us -> none  [the longest x1 10.6 us: gather_attention(): lax.all_gather(qkv_shard, 'fsdp', axis=0, tiled=True)]
    reshape x0 -> x3, local copies, waits for them, and re-layouts: none -> 17.6 us  [the longest x1 11.2 us: layer_forward(): shaped = projected.reshape(slot_count, SEQ, 3, H, HD)]
    dot_general x2 -> x4, matrix products: 18.8 us -> 35.2 us  [slot_scores(): jnp.einsum('qhd,khd->hqk', queries, keys_all, preferred_element_type=jnp....]
    convert_element_type x4 -> x2, local copies, waits for them, and re-layouts: 7.33 us -> 16.9 us  [the longest x1 13 us: layer_backward(): grad_qkv.reshape(slot_count * SEQ, 3 * D).astype(jnp.bfloat16)]
    dot_general x2, matrix products: 14.5 us -> 5.28 us  [attend_backward(): jnp.einsum('hqk,qhd->khd', grad_scores, queries, preferred_element_type=j...]
    dot_general x2, matrix products: 10.1 us -> 16.9 us  [attend_backward(): jnp.einsum('hqk,qhd->khd', probs_low, grad_ctx, preferred_element_type=jn...]
  transfers between devices with their start and end apart: 5 -> 1, of which waited for: 3 -> 0; matrix products, arithmetic and copies ran while one was open for 20% -> 5% of each run, Pallas kernels for 0% -> 0%
where the time goes in v1:
time: 533 us; the launch traced here: 525 us
  matrix products  198 us (37%)
  Pallas kernels  105 us (20%)
  blocking collectives  72.4 us (14%)
  other arithmetic  68.3 us (13%)
  local copies, waits for them, and re-layouts  64.5 us (12%)
  between operations  15.1 us (3%)
    pallas_call x1, Pallas kernels, gather_call(): pl.pallas_call(functools.partial(plain, mats), out_shape=outs, in_specs=[...  105 us
    psum x1, blocking collectives, body(): summed = lax.psum(grad_slots.astype(jnp.bfloat16), 'dp')  60.9 us
    dot_general x4, matrix products, slot_scores(): jnp.einsum('qhd,khd->hqk', queries, keys_all, preferred_element_type=jnp....  35.2 us
    convert_element_type x2, other arithmetic, attend_backward(): grad_scores = (attn_probs * (grad_probs - row_inner)).astype(jnp.bfloat16)  23.1 us
    dot_general x2, matrix products, attend_backward(): jnp.einsum('qhd,khd->hqk', grad_ctx, values, preferred_element_type=jnp.f...  20.9 us
    dot_general x1, matrix products, layer_backward(): jnp.einsum('rd,fd->rf', grad_feed, down_weight, preferred_element_type=jn...  18.7 us
    dot_general x2, matrix products, attend_forward(): jnp.einsum('hqk,khd->qhd', attn_probs, values, preferred_element_type=jnp...  18.4 us
    reduce_sum x2, other arithmetic, attend_forward(): row_total = jnp.sum(exponent, axis=-1, keepdims=True)  18.3 us
  transfers between devices with their start and end apart: 1, of which 0 were waited for; matrix products, arithmetic and copies ran while one was open for 5% of the time, Pallas kernels for 0%

profile of v1, /device:TPU:0, one launch (start us, length us, event | category | flops | bytes accessed | tf_op | source)
XLA Modules:
  0.0 525.2 jit_solution(2402016252670126739)
XLA Ops:
  14.5 105.3 %shard_map.189 = (bf16[3072,1024]{1,0:T(8,128)(2,1)}, bf16[1024,1024]{1,0:T(8,128)(2,1)}, bf16[4096,1024]{1,0:T(8,128)(2,1)}, bf16[1024,4096]{1,0:T(8,128)(2,1)}) custom-call(bf16[192,512]{1,0:T(8,128)(2,1)} %bitcast.244, bf16[64,512]{1,0:T(8,128)(2,1)} %bitcast.245, bf16[256,512]{1,0:T(8,128)(2,1)} %bitcast.240, bf16[64,2048]{1,0:T(8,128)(2,1)} %bitcast.243), custom_call_target="tpu_custom_call" | custom-call | tf_op jit(solution)/shard_map/pallas_call | solution.py:178
  119.8 11.9 %fusion.49 = bf16[1024,3072]{0,1:T(8,128)(2,1)} fusion(f32[3072]{0:T(1024)S(1)} %pad_maximum_fusion, bf16[3072,1024]{1,0:T(8,128)(2,1)} %get-tuple-element.101, bf16[1024,1024]{1,0:T(8,128)(2,1)} %bitcast.249), kind=kOutput, calls=%fused_computation.75 | convolution fusion | flops 6448742400 | bytes 14692352 | tf_op jit(solution)/shard_map/dot_general | solution.py:306
  131.7 11.2 %reshape.367 = bf16[2,512,3,16,64]{1,0,4,3,2:T(2,128)(2,1)} reshape(bf16[1024,3072]{0,1:T(8,128)(2,1)} %fusion.49) | data formatting | bytes 12582912 | tf_op jit(solution)/shard_map/reshape | solution.py:308
  142.9 6.1 %fusion.117 = (bf16[2,512,1,16,64]{1,0,4,3,2:T(2,128)(2,1)S(1)}, bf16[2,512,1,16,64]{1,0,4,3,2:T(2,128)(2,1)S(1)}, bf16[2,512,1,16,64]{1,0,4,3,2:T(2,128)(2,1)S(1)}) fusion(bf16[2,512,3,16,64]{1,0,4,3,2:T(2,128)(2,1)} %reshape.367), kind=kLoop, calls=%fused_computation.197 | loop fusion | bytes 12582912 | tf_op jit(solution)/shard_map/slice | solution.py:310
  152.9 54.9 %while.22 = (s32[]{:T(128)}, bf16[2,512,16,64]{1,3,2,0:T(8,128)(2,1)}, f32[2,16,512]{2,1,0:T(8,128)S(1)}, bf16[2,512,16,64]{1,3,2,0:T(8,128)(2,1)}, s32[2,512]{1...) while((s32[]{:T(128)}, ...), condition=%wide.region_3.4_spmd, body=%wide.region_0.3_spmd.sunk | while | flops 1124852736 | bytes 56897640 | solution.py:309
  153.5 8.4 %fusion.152 = (f32[16,512]{1,0:T(8,128)S(1)}, f32[16,512,512]{1,2,0:T(8,128)}) fusion(pred[512,512]{0,1:T(8,128)(4,1)S(1)} %or_and_fusion.4, bf16[2,512,16,64]{1,3,2,0:T(8,128)(2,1)S(1)} %get-tuple-element.415, s32[]{:T(128)} %get-tuple-element.399, bf16[2,512,16,64]{1,3,2,0:T(8,128)(2,1)} %get-tuple-element.414), kind=kOutput, calls=%fused_computation.3.clone.1 | convolution fusion | flops 549445632 | bytes 19170304 | tf_op jit(solution)/shard_map/while/body/eval_jaxpr/qhd,khd->hqk/dot_general | solution.py:253
  161.9 9.2 %fusion.153 = f32[16,512]{1,0:T(8,128)S(1)} fusion(f32[16,512,512]{1,2,0:T(8,128)} %get-tuple-element.375, f32[16,512]{1,0:T(8,128)S(1)} %get-tuple-element.376, pred[512,512]{0,1:T(8,128)(4,1)S(1)} %or_and_fusion.4), kind=kLoop, calls=%fused_computation.4.clone.1 | loop fusion | flops 16769024 | bytes 17104896 | tf_op jit(solution)/shard_map/while/body/eval_jaxpr/reduce_sum | solution.py:264
  171.1 9.2 %bitcast_dynamic-update-slice_fusion.4 = bf16[2,512,16,64]{1,3,2,0:T(8,128)(2,1)} fusion(bf16[2,512,16,64]{1,3,2,0:T(8,128)(2,1)} %get-tuple-element.400, s32[]{:T(128)} %get-tuple-element.399, f32[16,512,512]{1,2,0:T(8,128)} %get-tuple-element.375, f32[16,512]{1,0:T(8,128)S(1)} %fusion.153, f32[16,512]{1,0:T(8,128)S(1)} %get-tuple-element.376, ...), kind=kOutput, calls=%fused_computation.6.clone.1 | convolution fusion | flops 557842432 | bytes 20251648 | tf_op jit(solution)/shard_map/while/body/eval_jaxpr/hqk,khd->qhd/dot_general | solution.py:266
  180.6 8.4 %fusion.152 = (f32[16,512]{1,0:T(8,128)S(1)}, f32[16,512,512]{1,2,0:T(8,128)}) fusion(pred[512,512]{0,1:T(8,128)(4,1)S(1)} %or_and_fusion.4, bf16[2,512,16,64]{1,3,2,0:T(8,128)(2,1)S(1)} %get-tuple-element.415, s32[]{:T(128)} %get-tuple-element.399, bf16[2,512,16,64]{1,3,2,0:T(8,128)(2,1)} %get-tuple-element.414), kind=kOutput, calls=%fused_computation.3.clone.1 | convolution fusion | flops 549445632 | bytes 19170304 | tf_op jit(solution)/shard_map/while/body/eval_jaxpr/qhd,khd->hqk/dot_general | solution.py:253
  189.0 9.2 %fusion.153 = f32[16,512]{1,0:T(8,128)S(1)} fusion(f32[16,512,512]{1,2,0:T(8,128)} %get-tuple-element.375, f32[16,512]{1,0:T(8,128)S(1)} %get-tuple-element.376, pred[512,512]{0,1:T(8,128)(4,1)S(1)} %or_and_fusion.4), kind=kLoop, calls=%fused_computation.4.clone.1 | loop fusion | flops 16769024 | bytes 17104896 | tf_op jit(solution)/shard_map/while/body/eval_jaxpr/reduce_sum | solution.py:264
  198.2 9.2 %bitcast_dynamic-update-slice_fusion.4 = bf16[2,512,16,64]{1,3,2,0:T(8,128)(2,1)} fusion(bf16[2,512,16,64]{1,3,2,0:T(8,128)(2,1)} %get-tuple-element.400, s32[]{:T(128)} %get-tuple-element.399, f32[16,512,512]{1,2,0:T(8,128)} %get-tuple-element.375, f32[16,512]{1,0:T(8,128)S(1)} %fusion.153, f32[16,512]{1,0:T(8,128)S(1)} %get-tuple-element.376, ...), kind=kOutput, calls=%fused_computation.6.clone.1 | convolution fusion | flops 557842432 | bytes 20251648 | tf_op jit(solution)/shard_map/while/body/eval_jaxpr/hqk,khd->qhd/dot_general | solution.py:266
  215.7 15.6 %fusion.58 = f32[1024,4096]{1,0:T(8,128)} fusion(bf16[4096,1024]{1,0:T(8,128)(2,1)} %get-tuple-element.104, f32[1024,1024]{1,0:T(8,128)S(1)} %get-tuple-element.259, f32[1024]{0:T(1024)S(1)} %copy-done.26, f32[1024]{0:T(1024)S(1)} %copy-done.18, f32[1024]{0:T(1024)S(1)} %add_rsqrt_fusion.1, f32[1024]{0:T(1024)S(1)} %broadcast_multiply_fusion.6), kind=kOutput, calls=%fused_computation.103 | convolution fusion | flops 8595177472 | bytes 29376512 | tf_op jit(solution)/shard_map/dot_general | solution.py:318
  231.3 17.5 %fusion.121 = (f32[1024]{0:T(1024)S(1)}, f32[1024,1024]{1,0:T(8,128)}) fusion(f32[1024]{0:T(1024)S(1)} %copy-done.25, bf16[1024,4096]{1,0:T(8,128)(2,1)} %get-tuple-element.105, f32[1024,4096]{1,0:T(8,128)} %fusion.58, f32[4096]{0:T(1024)S(1)} %copy-done.21, f32[1024]{0:T(1024)S(1)} %copy-done.26, f32[1024]{0:T(1024)S(1)} %copy-done.18, ...), kind=kOutput, calls=%fused_computation.201 | convolution fusion | flops 8622439424 | bytes 33595392 | tf_op jit(solution)/shard_map/dot_general | solution.py:320
  261.0 18.7 %convert_reduce_fusion = (f32[4096]{0:T(1024)}, bf16[1024,4096]{1,0:T(8,128)(2,1)}) fusion(f32[1024,4096]{1,0:T(8,128)} %fusion.58, f32[4096]{0:T(1024)S(1)} %copy-done.21, bf16[1024,4096]{1,0:T(8,128)(2,1)S(1)} %bitcast.248, f32[1024,1024]{1,0:T(8,128)S(1)} %get-tuple-element.235), kind=kOutput, calls=%fused_computation.67 | convolution fusion | flops 8645505024 | bytes 37781504 | tf_op jit(solution)/shard_map/rd,fd->rf/dot_general | solution.py:348
  279.7 15.8 %multiply_reduce_fusion.1 = (f32[1024]{0:T(1024)}, f32[1024]{0:T(1024)S(1)}, f32[1024]{0:T(1024)S(1)}, f32[1024]{0:T(1024)}, f32[1024,1024]{1,0:T(8,128)S(1)}) fusion(f32[1024,1024]{1,0:T(8,128)S(1)} %copy-done.7, f32[1024]{0:T(1024)S(1)} %add_rsqrt_fusion.1, f32[1024]{0:T(1024)S(1)} %broadcast_multiply_fusion.6, f32[1024]{0:T(1024)S(1)} %copy-done.18, ...), kind=kOutput, calls=%fused_computation.87 | convolution fusion | flops 8600416256 | bytes 29388800 | tf_op jit(solution)/shard_map/rf,df->rd/dot_general | solution.py:351
  303.1 6.4 %reshape.387 = bf16[2,512,16,64]{3,2,1,0:T(8,128)(2,1)} reshape(bf16[1024,1024]{1,0:T(8,128)(2,1)} %convolution_convert_fusion) | data formatting | bytes 4194304 | tf_op jit(solution)/shard_map/reshape | solution.py:362
  309.5 5.4 %copy.120 = bf16[2,512,16,64]{1,3,2,0:T(8,128)(2,1)} copy(bf16[2,512,16,64]{3,2,1,0:T(8,128)(2,1)} %reshape.387) | data formatting | bytes 4194304 | tf_op jit(solution)/shard_map/while | solution.py:363
  314.9 92.5 %while.23 = (s32[]{:T(128)}, bf16[2,512,3,16,64]{1,4,3,2,0:T(8,128)(2,1)}, bf16[2,512,16,64]{1,3,2,0:T(8,128)(2,1)S(1)}, s32[2,512]{1,0:T(2,128)S(1)}, s32[2,512...) while((s32[]{:T(128)}, ...), condition=%wide.region_14.15_spmd, body=%wide.region_12.14_spmd.sunk | while | flops 2734416896 | bytes 168473280 | solution.py:363
  315.5 9.2 %subtract_exponential_fusion.3 = f32[16,512,512]{1,2,0:T(8,128)} fusion(f32[16,512]{1,0:T(8,128)S(1)} %dynamic-slice_bitcast_fusion.2, pred[512,512]{0,1:T(8,128)(4,1)S(1)} %or_and_fusion.5, bf16[2,512,16,64]{1,3,2,0:T(8,128)(2,1)} %get-tuple-element.442, s32[]{:T(128)} %get-tuple-element.427, bf16[2,512,16,64]{1,3,2,0:T(8,128)(2,1)S(1)} %get-tuple-element.439), kind=kOutput, calls=%fused_computation.26.clone.1 | convolution fusion | flops 549453824 | bytes 19170304 | tf_op jit(solution)/shard_map/while/body/eval_jaxpr/qhd,khd->hqk/dot_general | solution.py:253
  324.7 10.4 %multiply_reduce_fusion.7 = (f32[16,512]{1,0:T(8,128)S(1)}, f32[16,512,512]{1,2,0:T(8,128)}) fusion(f32[16,512,512]{1,2,0:T(8,128)} %subtract_exponential_fusion.3, bf16[2,512,16,64]{1,3,2,0:T(8,128)(2,1)S(1)} %copy-done.4, s32[]{:T(128)} %get-tuple-element.427, bf16[2,512,16,64]{1,3,2,0:T(8,128)(2,1)S(1)} %copy-done.2), kind=kOutput, calls=%fused_computation.25.clone.1 | convolution fusion | flops 545251328 | bytes 35685376 | tf_op jit(solution)/shard_map/while/body/eval_jaxpr/qhd,khd->hqk/dot_general | solution.py:275
  335.2 11.6 %multiply_convert_fusion.6 = bf16[16,512,512]{1,2,0:T(8,128)(2,1)S(1)} fusion(f32[16,512,512]{1,2,0:T(8,128)} %subtract_exponential_fusion.3, f32[16,512,512]{1,2,0:T(8,128)} %get-tuple-element.388, f32[16,512]{1,0:T(8,128)S(1)} %get-tuple-element.389), kind=kLoop, calls=%fused_computation.24.clone.1 | loop fusion | flops 12582912 | bytes 41975808 | tf_op jit(solution)/shard_map/while/body/eval_jaxpr/convert_element_type | solution.py:277
  351.0 8.5 %fusion.162 = bf16[512,1,16,64]{0,3,2,1:T(8,128)(2,1)S(1)} fusion(f32[16,512,512]{1,2,0:T(8,128)} %subtract_exponential_fusion.3, bf16[2,512,16,64]{1,3,2,0:T(8,128)(2,1)S(1)} %copy-done.2, s32[]{:T(128)} %get-tuple-element.427), kind=kOutput, calls=%fused_computation.33.clone.1 | convolution fusion | flops 541065216 | bytes 18874372 | tf_op jit(solution)/shard_map/while/body/eval_jaxpr/hqk,qhd->khd/dot_general | solution.py:284
  361.7 9.2 %subtract_exponential_fusion.3 = f32[16,512,512]{1,2,0:T(8,128)} fusion(f32[16,512]{1,0:T(8,128)S(1)} %dynamic-slice_bitcast_fusion.2, pred[512,512]{0,1:T(8,128)(4,1)S(1)} %or_and_fusion.5, bf16[2,512,16,64]{1,3,2,0:T(8,128)(2,1)} %get-tuple-element.442, s32[]{:T(128)} %get-tuple-element.427, bf16[2,512,16,64]{1,3,2,0:T(8,128)(2,1)S(1)} %get-tuple-element.439), kind=kOutput, calls=%fused_computation.26.clone.1 | convolution fusion | flops 549453824 | bytes 19170304 | tf_op jit(solution)/shard_map/while/body/eval_jaxpr/qhd,khd->hqk/dot_general | solution.py:253
  370.9 10.4 %multiply_reduce_fusion.7 = (f32[16,512]{1,0:T(8,128)S(1)}, f32[16,512,512]{1,2,0:T(8,128)}) fusion(f32[16,512,512]{1,2,0:T(8,128)} %subtract_exponential_fusion.3, bf16[2,512,16,64]{1,3,2,0:T(8,128)(2,1)S(1)} %copy-done.4, s32[]{:T(128)} %get-tuple-element.427, bf16[2,512,16,64]{1,3,2,0:T(8,128)(2,1)S(1)} %copy-done.2), kind=kOutput, calls=%fused_computation.25.clone.1 | convolution fusion | flops 545251328 | bytes 35685376 | tf_op jit(solution)/shard_map/while/body/eval_jaxpr/qhd,khd->hqk/dot_general | solution.py:275
  381.3 11.6 %multiply_convert_fusion.6 = bf16[16,512,512]{1,2,0:T(8,128)(2,1)S(1)} fusion(f32[16,512,512]{1,2,0:T(8,128)} %subtract_exponential_fusion.3, f32[16,512,512]{1,2,0:T(8,128)} %get-tuple-element.388, f32[16,512]{1,0:T(8,128)S(1)} %get-tuple-element.389), kind=kLoop, calls=%fused_computation.24.clone.1 | loop fusion | flops 12582912 | bytes 41975808 | tf_op jit(solution)/shard_map/while/body/eval_jaxpr/convert_element_type | solution.py:277
  397.1 8.5 %fusion.162 = bf16[512,1,16,64]{0,3,2,1:T(8,128)(2,1)S(1)} fusion(f32[16,512,512]{1,2,0:T(8,128)} %subtract_exponential_fusion.3, bf16[2,512,16,64]{1,3,2,0:T(8,128)(2,1)S(1)} %copy-done.2, s32[]{:T(128)} %get-tuple-element.427), kind=kOutput, calls=%fused_computation.33.clone.1 | convolution fusion | flops 541065216 | bytes 18874372 | tf_op jit(solution)/shard_map/while/body/eval_jaxpr/hqk,qhd->khd/dot_general | solution.py:284
  412.8 13.0 %copy.121 = bf16[2,512,3,16,64]{1,0,4,3,2:T(2,128)(2,1)} copy(bf16[2,512,3,16,64]{1,4,3,2,0:T(8,128)(2,1)} %get-tuple-element.107) | data formatting | bytes 12582912 | tf_op jit(solution)/shard_map/convert_element_type | solution.py:375
  425.8 5.0 copy.156
  430.8 9.8 %add_convert_fusion.1 = bf16[1024,1024]{1,0:T(8,128)(2,1)} fusion(f32[1024,1024]{1,0:T(8,128)S(1)} %copy-done.9, bf16[1024,3072]{0,1:T(8,128)(2,1)S(1)} %bitcast.236, bf16[3072,1024]{1,0:T(8,128)(2,1)} %get-tuple-element.101), kind=kOutput, calls=%fused_computation.90 | convolution fusion | flops 6444548096 | bytes 18874368 | tf_op jit(solution)/shard_map/re,de->rd/dot_general | solution.py:377
  441.1 60.9 %psum.8 = bf16[1,6,32,32]{3,2,1,0:T(8,128)(2,1)S(1)} all-reduce(bf16[1,6,32,32]{3,2,1,0:T(8,128)(2,1)} %reduce-scatter.2.cloned.1.call-done), channel_id=1, replica_groups=mesh['dp'=16,'fsdp'=2] {'dp'}, use_global_device_ids=true, to_apply=%region_24.25 | all-reduce | flops 6144 | bytes 24576 | tf_op jit(solution)/shard_map/psum | solution.py:462
  503.9 6.2 %all-gather = f32[12,32,32]{2,1,0:T(8,128)S(1)} all-gather(f32[6,32,32]{2,1,0:T(8,128)S(1)} %fusion.65), channel_id=2, replica_groups=mesh['dp'=16,'fsdp'=2] {'fsdp'}, dimensions={0}, use_global_device_ids=true | all-gather | bytes 73728 | tf_op jit(solution)/shard_map/all_gather | solution.py:479
  511.4 5.3 %all_gather.6 = f32[2,6,32,32]{3,2,1,0:T(8,128)S(1)} all-gather(f32[1,6,32,32]{3,2,1,0:T(8,128)S(1)} %convert_element_type.128), channel_id=1, replica_groups=mesh['dp'=16,'fsdp'=2] {'fsdp'}, dimensions={0}, use_global_device_ids=true | all-gather | bytes 73728 | tf_op jit(solution)/shard_map/all_gather | solution.py:478
  (173 shorter events, 62.2 us)
Async XLA Ops:
  7.2 495.2 %copy-start = (f32[1,6,32,32]{3,2,1,0:T(8,128)S(1)}, f32[1,6,32,32]{3,2,1,0:T(8,128)}, u32[]{:S(2)}) copy-start(f32[1,6,32,32]{3,2,1,0:T(8,128)} %param.30) | copy-start | bytes 73732
  7.2 433.9 %reduce-scatter.2.cloned.1.call-start = ((), (), s32[]{:S(2)}) async-start(), calls=%async_computation.1 | async-start | bytes 147456 | tf_op jit(solution)/shard_map/reduce_scatter | solution.py:463
  207.8 4.5 copy-start.27
  207.8 4.5 copy-start.32
  207.9 4.5 copy-start.33
  214.9 16.3 %copy-start.6 = (f32[1024,1024]{1,0:T(8,128)}, f32[1024,1024]{1,0:T(8,128)S(1)}, u32[]{:S(2)}) copy-start(f32[1024,1024]{1,0:T(8,128)S(1)} %get-tuple-element.259) | copy-start | bytes 12582916
  215.7 15.6 %copy-start.21 = (f32[4096]{0:T(1024)S(1)}, f32[4096]{0:T(1024)}, u32[]{:S(2)}) copy-start(f32[4096]{0:T(1024)} %slice.61) | copy-start | bytes 49156
  215.7 15.6 %copy-start.25 = (f32[1024]{0:T(1024)S(1)}, f32[1024]{0:T(1024)}, u32[]{:S(2)}) copy-start(f32[1024]{0:T(1024)} %get-tuple-element.249) | copy-start | bytes 12292
  231.3 20.4 %copy-start.15 = (f32[1024]{0:T(1024)S(1)}, f32[1024]{0:T(1024)}, u32[]{:S(2)}) copy-start(f32[1024]{0:T(1024)} %get-tuple-element.248) | copy-start | bytes 12292
  248.8 6.3 %copy-start.3 = (f32[1024,1024]{1,0:T(8,128)S(1)}, f32[1024,1024]{1,0:T(8,128)}, u32[]{:S(2)}) copy-start(f32[1024,1024]{1,0:T(8,128)} %get-tuple-element.261) | copy-start | bytes 12582916
  248.8 6.3 %copy-start.5 = (bf16[2,1,512,1024]{3,2,1,0:T(8,128)(2,1)S(1)}, bf16[2,1,512,1024]{3,2,1,0:T(8,128)(2,1)}, u32[]{:S(2)}) copy-start(bf16[2,1,512,1024]{3,2,1,0:T(8,128)(2,1)} %param.19) | copy-start | bytes 6291460
  251.7 5.9 %copy-start.16 = (f32[1024]{0:T(1024)S(1)}, f32[1024]{0:T(1024)}, u32[]{:S(2)}) copy-start(f32[1024]{0:T(1024)} %get-tuple-element.255) | copy-start | bytes 12292
  255.1 6.0 %slice-start = ((s8[8388608]{0:T(1024)(128)(4,1)}), s8[4194304]{0:T(1024)(128)(4,1)S(1)}, s32[]{:S(2)}) async-start(s8[8388608]{0:T(1024)(128)(4,1)} %bitcast.247), calls=%async_computation.2 | async-start | bytes 8388608
  261.0 18.7 %copy-start.7 = (f32[1024,1024]{1,0:T(8,128)S(1)}, f32[1024,1024]{1,0:T(8,128)}, u32[]{:S(2)}) copy-start(f32[1024,1024]{1,0:T(8,128)} %copy-done.6) | copy-start | bytes 12582916
  315.5 9.2 %copy-start.2 = (bf16[2,512,16,64]{1,3,2,0:T(8,128)(2,1)S(1)}, bf16[2,512,16,64]{1,3,2,0:T(8,128)(2,1)}, u32[]{:S(2)}) copy-start(bf16[2,512,16,64]{1,3,2,0:T(8,128)(2,1)} %get-tuple-element.444) | copy-start | bytes 6291460 | tf_op jit(solution)/shard_map/while
  315.5 9.2 %copy-start.4 = (bf16[2,512,16,64]{1,3,2,0:T(8,128)(2,1)S(1)}, bf16[2,512,16,64]{1,3,2,0:T(8,128)(2,1)}, u32[]{:S(2)}) copy-start(bf16[2,512,16,64]{1,3,2,0:T(8,128)(2,1)} %get-tuple-element.445) | copy-start | bytes 6291460 | tf_op jit(solution)/shard_map/while
  361.7 9.2 %copy-start.2 = (bf16[2,512,16,64]{1,3,2,0:T(8,128)(2,1)S(1)}, bf16[2,512,16,64]{1,3,2,0:T(8,128)(2,1)}, u32[]{:S(2)}) copy-start(bf16[2,512,16,64]{1,3,2,0:T(8,128)(2,1)} %get-tuple-element.444) | copy-start | bytes 6291460 | tf_op jit(solution)/shard_map/while
  361.7 9.2 %copy-start.4 = (bf16[2,512,16,64]{1,3,2,0:T(8,128)(2,1)S(1)}, bf16[2,512,16,64]{1,3,2,0:T(8,128)(2,1)}, u32[]{:S(2)}) copy-start(bf16[2,512,16,64]{1,3,2,0:T(8,128)(2,1)} %get-tuple-element.445) | copy-start | bytes 6291460 | tf_op jit(solution)/shard_map/while
  407.4 3.9 copy-start.22
  407.4 4.0 copy-start.17
  407.4 4.0 copy-start.29
  407.4 4.0 copy-start.28
  407.4 4.0 copy-start.23
  407.4 4.0 copy-start.19
  407.5 4.1 copy-start.35
  407.5 4.1 copy-start.24
  407.5 5.2 copy-start.11
  425.8 5.0 copy-start.9
  430.8 71.3 %copy-start.14 = (f32[1,6,32,32]{3,2,1,0:T(8,128)S(1)}, f32[1,6,32,32]{3,2,1,0:T(8,128)}, u32[]{:S(2)}) copy-start(f32[1,6,32,32]{3,2,1,0:T(8,128)} %param.29) | copy-start | bytes 73732
  430.8 71.6 %copy-start.12 = (f32[1,6,32,32]{3,2,1,0:T(8,128)S(1)}, f32[1,6,32,32]{3,2,1,0:T(8,128)}, u32[]{:S(2)}) copy-start(f32[1,6,32,32]{3,2,1,0:T(8,128)} %param.28) | copy-start | bytes 73732
  430.8 71.6 %copy-start.13 = (f32[1,6,32,32]{3,2,1,0:T(8,128)S(1)}, f32[1,6,32,32]{3,2,1,0:T(8,128)}, u32[]{:S(2)}) copy-start(f32[1,6,32,32]{3,2,1,0:T(8,128)} %param.27) | copy-start | bytes 73732
  510.7 7.1 %copy-start.10 = (f32[12288]{0:T(1024)}, f32[12288]{0:T(1024)S(1)}, u32[]{:S(2)}) copy-start(f32[12288]{0:T(1024)S(1)} %reshape.379) | copy-start | bytes 147460
  (10 other events, 22.2 us)
Sparse Core Ops, SparseCore 0:
  412.8 8.5 reduce-scatter.1
